TPU v7x, 32 devices: a whole 2x2x4 slice. The times are simulated.
32 devices in a mesh: groups: 2 (over y), seq: 16 (over z, x, core).
Axes of the slice: x: 2, y: 2, z: 4, core: 2. Of those that a mesh axis runs over, the one named last changes fastest.
Arguments:
- visible_tokens: bfloat16 [1024, 1280], P(('groups', 'seq')), parts along dimension 0, may hold values from -6 to 6
- restore_order: int32 [4096], P(('groups', 'seq')), parts along dimension 0, may hold values from 0 to 2047, as said below
- encoder_project: bfloat16 [1280, 1920], replicated, may hold values from -6 to 6
- encoder_output: bfloat16 [640, 1280], replicated, may hold values from -0.25 to 0.25
- decoder_embed: bfloat16 [1280, 512], replicated, may hold values from -0.15625 to 0.15625
- mask_token: bfloat16 [512], replicated, may hold values from -1.5 to 1.5
- position_table: bfloat16 [2048, 512], P('seq'), may hold values from -4.5 to 4.5
- decoder_project: bfloat16 [512, 768], replicated, may hold values from -6 to 6
- decoder_output: bfloat16 [256, 512], replicated, may hold values from -0.375 to 0.375
- expand_weight: bfloat16 [512, 2048], replicated, may hold values from -0.25 to 0.25
- shrink_weight: bfloat16 [2048, 512], replicated, may hold values from -0.125 to 0.125
Outputs:
- latent: bfloat16 [1024, 1280], P(('groups', 'seq')), parts along dimension 0
- decoded: bfloat16 [4096, 512], P(('groups', 'seq')), parts along dimension 0
There are 2 independent parts, one for each index of `groups`. A program takes and returns all parts, laid end to end along the dimension named above; an argument that names none is the same for every part. Nothing has to cross between parts.
Inputs may be any that keep to these rules, and one draw needn't show every extreme that they name: `restore_order`: a permutation of the patch numbers; every device's 128 patches hold exactly 32 ranks under 512, and of the ranks r with the same r // 32, a device's patches hold either none or exactly 2.
All inputs are finite; a program needn't handle non-finite values.
Results may differ from a plain program's by a relative error of at most 0.0095.
Values may be sent and summed in bfloat16 or wider, within the bound.
A program may use at most 128 MiB of HBM per device.

v0:
```python
import jax
import jax.numpy as jnp
from jax import lax
from jax.sharding import PartitionSpec as P

EH = 8
DH = 8


def normalize(values):
    values = values.astype(jnp.float32)
    centre = values - jnp.mean(values, -1, keepdims=True)
    spread = jnp.mean(centre * centre, -1, keepdims=True)
    return (centre * lax.rsqrt(spread + 1e-06)).astype(jnp.bfloat16)


def attend(queries, keys, values, heads):
    total, width = queries.shape
    size = width // heads
    query_heads = queries.reshape(total, heads, size).transpose(1, 0, 2)
    key_heads = keys.reshape(keys.shape[0], heads, size).transpose(1, 0, 2)
    value_heads = values.reshape(values.shape[0], heads, size).transpose(1, 0, 2)

    def one_head(operands):
        query_part, key_part, value_part = operands
        scores = lax.dot_general(
            query_part, key_part, (((1,), (1,)), ((), ())), preferred_element_type=jnp.float32
        ) * size ** (-0.5)
        highest = jnp.max(scores, -1, keepdims=True)
        powers = jnp.exp(scores - highest)
        weights = (powers / jnp.sum(powers, -1, keepdims=True)).astype(jnp.bfloat16)
        return jnp.dot(weights, value_part, preferred_element_type=jnp.float32).astype(jnp.bfloat16)

    result = lax.map(one_head, (query_heads, key_heads, value_heads))
    return result.transpose(1, 0, 2).reshape(total, width)


def on_device(
    visible_tokens,
    restore_order,
    encoder_project,
    encoder_output,
    decoder_embed,
    mask_token,
    position_table,
    decoder_project,
    decoder_output,
    expand_weight,
    shrink_weight,
):
    enc_width = encoder_output.shape[0]
    dec_width = decoder_output.shape[0]
    enc_act = jnp.dot(
        normalize(visible_tokens), encoder_project, preferred_element_type=jnp.float32
    ).astype(jnp.bfloat16)
    enc_pairs = lax.all_gather(enc_act[:, enc_width:], "seq", axis=0, tiled=True)
    enc_mix = attend(enc_act[:, :enc_width], enc_pairs[:, :enc_width], enc_pairs[:, enc_width:], EH)
    latent = (
        visible_tokens.astype(jnp.float32)
        + jnp.dot(enc_mix, encoder_output, preferred_element_type=jnp.float32)
    ).astype(jnp.bfloat16)
    peers = lax.axis_size("seq")
    vis_rows = latent.shape[0]
    visible_count = vis_rows * peers
    seen = restore_order < visible_count
    chosen = jnp.minimum(restore_order, visible_count - 1)
    local_embedded = jnp.dot(
        normalize(latent), decoder_embed, preferred_element_type=jnp.float32
    ).astype(jnp.bfloat16)
    capacity = max(1, vis_rows // peers)
    owners = chosen // vis_rows
    offsets = chosen % vis_rows
    owner_hot = (
        (owners[:, None] == jnp.arange(peers, dtype=jnp.int32)[None, :]) & seen[:, None]
    ).astype(jnp.int32)
    earlier = jnp.cumsum(owner_hot, axis=0) - owner_hot
    slot_index = jnp.sum(earlier * owner_hot, axis=1)
    flat_slot = owners * capacity + slot_index
    target_hot = (
        flat_slot[:, None] == jnp.arange(peers * capacity, dtype=jnp.int32)[None, :]
    ) & seen[:, None]
    requests = jnp.max(jnp.where(target_hot, offsets[:, None], -1), axis=0).reshape(peers, capacity)
    asked = lax.all_to_all(requests, "seq", split_axis=0, concat_axis=0, tiled=True)
    answers = jnp.take(local_embedded, jnp.maximum(asked, 0).reshape(-1), axis=0).reshape(
        peers, capacity, local_embedded.shape[1]
    )
    replies = lax.all_to_all(answers, "seq", split_axis=0, concat_axis=0, tiled=True)
    replies = replies.reshape(peers * capacity, local_embedded.shape[1])
    picked = jnp.take(replies, jnp.minimum(flat_slot, peers * capacity - 1), axis=0)
    filled = jnp.where(
        seen[:, None], picked.astype(jnp.float32), mask_token.astype(jnp.float32)[None, :]
    )
    dec_in = (filled + position_table.astype(jnp.float32)).astype(jnp.bfloat16)
    dec_act = jnp.dot(
        normalize(dec_in), decoder_project, preferred_element_type=jnp.float32
    ).astype(jnp.bfloat16)
    dec_pairs = lax.all_gather(dec_act[:, dec_width:], "seq", axis=0, tiled=True)
    dec_mix = attend(dec_act[:, :dec_width], dec_pairs[:, :dec_width], dec_pairs[:, dec_width:], DH)
    middle = (
        dec_in.astype(jnp.float32)
        + jnp.dot(dec_mix, decoder_output, preferred_element_type=jnp.float32)
    ).astype(jnp.bfloat16)
    hidden = jax.nn.gelu(
        jnp.dot(normalize(middle), expand_weight, preferred_element_type=jnp.float32),
        approximate=False,
    ).astype(jnp.bfloat16)
    decoded = (
        middle.astype(jnp.float32)
        + jnp.dot(hidden, shrink_weight, preferred_element_type=jnp.float32)
    ).astype(jnp.bfloat16)
    return (latent, decoded)


def solution(mesh):
    in_specs = (
        P(("groups", "seq"), None),
        P(("groups", "seq")),
        P(),
        P(),
        P(),
        P(),
        P("seq", None),
        P(),
        P(),
        P(),
        P(),
    )
    out_specs = (P(("groups", "seq"), None), P(("groups", "seq"), None))
    return jax.shard_map(
        on_device, mesh=mesh, in_specs=in_specs, out_specs=out_specs, check_vma=False
    )
```

profile of v0, /device:TPU:1, one launch (start us, length us, event | category | flops | bytes accessed | tf_op | source)
XLA Modules:
  0.0 183.7 jit_solution(6671788714258623654)
XLA Ops:
  9.5 3.4 %convolution_convert_fusion.2 = bf16[32,1920]{1,0:T(8,128)(2,1)S(1)} fusion(bf16[1280,1920]{1,0:T(8,128)(2,1)} %param.17, bf16[32,1280]{1,0:T(8,128)(2,1)} %param.15, f32[32]{0:T(128)S(1)} %add_rsqrt_fusion.3, f32[32]{0:T(128)S(1)} %broadcast_multiply_fusion.3), kind=kOutput, calls=%fused_computation.36 | convolution fusion | flops 157511680 | bytes 5120256 | tf_op jit(solution)/shard_map/dot_general | solution.py:53
  14.9 7.3 %all-to-all-start = ((s32[16,1,2]{2,1,0:T(1,128)}), s32[16,1,2]{2,1,0:T(1,128)S(1)}, u32[]{:S(2)}, u32[]{:S(2)}) async-start(s32[16,1,2]{2,1,0:T(1,128)} %bitcast.14), calls=%async_computation | async-start | bytes 16384 | tf_op jit(solution)/shard_map/all_to_all | solution.py:83
  23.0 5.0 %all-to-all-done = s32[16,1,2]{2,1,0:T(1,128)S(1)} async-done(((s32[16,1,2]{2,1,0:T(1,128)}), s32[16,1,2]{2,1,0:T(1,128)S(1)}, u32[]{:S(2)}, u32[]{:S(2)}) %all-to-all-start) | async-done | bytes 160 | tf_op jit(solution)/shard_map/all_to_all | solution.py:83
  28.4 26.7 %all-gather.3.cloned.1.call-done = bf16[512,1280]{1,0:T(8,128)(2,1)} async-done(((bf16[32,1280]{1,0:T(8,128)(2,1)}), bf16[512,1280]{1,0:T(8,128)(2,1)}) %all-gather.3.cloned.1.call-update) | async-done | bytes 1310736 | tf_op jit(solution)/shard_map/all_gather | solution.py:56
  57.9 22.7 %while.20 = (s32[]{:T(128)}, bf16[8,32,80]{2,1,0:T(8,128)(2,1)}, bf16[8,32,80]{2,1,0:T(8,128)(2,1)}, bf16[8,512,80]{1,2,0:T(8,128)(2,1)S(1)}, bf16[8,512,80]{1,2,0:T(8,128)(2,1)}, /*index=5*/s32[]{:T(128)}) while((s32[]{:T(128)}, bf16[8,32,80]{2,1,0:T(8,128)(2,1)}, bf16[8,32,80]{2,1,0:T(8,128)(2,1)}, bf16[8,512,80]{1,2,0:T(8,128)(2,1)S(1)}, ...), condition=%wide.region_5.6_spmd, body=%wide.region_2.5_spmd.sunk | while | flops 5360066 | bytes 379597 | solution.py:34
  59.0 1.7 fusion.153
  61.8 1.7 fusion.153
  64.7 1.7 fusion.153
  67.5 1.7 fusion.153
  70.4 1.7 fusion.153
  73.2 1.7 fusion.153
  76.0 1.7 fusion.153
  78.9 1.7 fusion.153
  80.6 1.6 copy.55
  82.2 1.6 reshape.131
  83.8 1.9 %convert_reduce_fusion.2 = (f32[32]{0:T(128)S(1)}, bf16[32,1280]{1,0:T(8,128)(2,1)S(1)}) fusion(bf16[32,640]{1,0:T(8,128)(2,1)} %reshape.131, bf16[640,1280]{1,0:T(8,128)(2,1)} %param.18, bf16[32,1280]{1,0:T(8,128)(2,1)S(1)} %copy-done.2), kind=kOutput, calls=%fused_computation.105 | convolution fusion | flops 52633568 | bytes 1843328 | tf_op jit(solution)/shard_map/dot_general | solution.py:60
  88.1 3.7 %all-to-all-start.1 = ((bf16[16,2,512]{2,1,0:T(2,128)(2,1)}), bf16[16,2,512]{2,1,0:T(2,128)(2,1)S(1)}, u32[]{:S(2)}, u32[]{:S(2)}) async-start(bf16[16,2,512]{2,1,0:T(2,128)(2,1)} %broadcast_select_fusion), calls=%async_computation.1 | async-start | bytes 65536 | tf_op jit(solution)/shard_map/all_to_all | solution.py:87
  91.8 5.9 %all-to-all-done.1 = bf16[16,2,512]{2,1,0:T(2,128)(2,1)S(1)} async-done(((bf16[16,2,512]{2,1,0:T(2,128)(2,1)}), bf16[16,2,512]{2,1,0:T(2,128)(2,1)S(1)}, u32[]{:S(2)}, u32[]{:S(2)}) %all-to-all-start.1) | async-done | bytes 32800 | tf_op jit(solution)/shard_map/all_to_all | solution.py:87
  99.9 1.4 convolution_convert_fusion.3
  102.1 39.2 %all-gather.5.cloned.1.call-done = bf16[2048,512]{1,0:T(8,128)(2,1)} async-done(((bf16[128,512]{1,0:T(8,128)(2,1)}), bf16[2048,512]{1,0:T(8,128)(2,1)}) %all-gather.5.cloned.1.call-update) | async-done | bytes 2097168 | tf_op jit(solution)/shard_map/all_gather | solution.py:97
  141.4 2.7 %fusion.130 = (bf16[2048,256]{1,0:T(8,128)(2,1)}, bf16[2048,256]{1,0:T(8,128)(2,1)S(1)}) fusion(bf16[2048,512]{1,0:T(8,128)(2,1)} %all-gather.5.cloned.1.call-done), kind=kLoop, calls=%fused_computation.185 | loop fusion | bytes 4194304 | tf_op jit(solution)/shard_map/slice | solution.py:98
  144.0 2.3 %copy.61 = bf16[2048,256]{0,1:T(8,128)(2,1)} copy(bf16[2048,256]{1,0:T(8,128)(2,1)} %get-tuple-element.119) | data formatting | bytes 2097152 | tf_op jit(solution)/shard_map/slice | solution.py:98
  147.7 23.3 %while.21 = (s32[]{:T(128)}, bf16[8,128,32]{1,2,0:T(8,128)(2,1)S(1)}, bf16[8,128,32]{1,2,0:T(8,128)(2,1)S(1)}, bf16[8,2048,32]{1,2,0:T(8,128)(2,1)}, bf16[8,2048,32]{1,2,0:T(8,128)(2,1)}, /*index=5*/s32[]{:T(128)}) while((s32[]{:T(128)}, bf16[8,128,32]{1,2,0:T(8,128)(2,1)S(1)}, bf16[8,128,32]{1,2,0:T(8,128)(2,1)S(1)}, ...), condition=%wide.region_16.17_spmd, body=%wide.region_13.16_spmd.sunk | while | flops 35393280 | bytes 3428941 | solution.py:34
  171.6 5.3 %fusion.27 = bf16[128,512]{1,0:T(8,128)(2,1)} fusion(f32[128,512]{1,0:T(8,128)S(1)} %get-tuple-element.126, bf16[2048,512]{1,0:T(8,128)(2,1)S(1)} %copy-done, bf16[512,2048]{1,0:T(8,128)(2,1)} %param.24, f32[128]{0:T(128)S(1)} %add_rsqrt_fusion, f32[128]{0:T(128)S(1)} %broadcast_multiply_fusion), kind=kOutput, calls=%fused_computation.43 | convolution fusion | flops 554237952 | bytes 4588544 | tf_op jit(solution)/shard_map/dot_general | solution.py:109
  (109 shorter events, 47.6 us)
Async XLA Ops:
  7.2 164.4 %copy-start = (bf16[2048,512]{1,0:T(8,128)(2,1)S(1)}, bf16[2048,512]{1,0:T(8,128)(2,1)}, u32[]{:S(2)}) copy-start(bf16[2048,512]{1,0:T(8,128)(2,1)} %param.25) | copy-start | bytes 6291460
  7.2 47.9 %all-gather.3.cloned.1.call-start = ((), (), s32[]{:S(2)}) async-start(), calls=%async_computation.2 | async-start | bytes 1392640 | tf_op jit(solution)/shard_map/all_gather | solution.py:56
  9.5 4.1 %copy-start.6 = (s32[128]{0:T(128)S(1)}, s32[128]{0:T(128)}, u32[]{:S(2)}) copy-start(s32[128]{0:T(128)} %param.16) | copy-start | bytes 1540
  9.5 12.8 %copy-start.5 = (bf16[512]{0:T(512)(128)(2,1)S(1)}, bf16[512]{0:T(512)(128)(2,1)}, u32[]{:S(2)}) copy-start(bf16[512]{0:T(512)(128)(2,1)} %param.20) | copy-start | bytes 3076
  14.9 13.1 %all-to-all-start = ((s32[16,1,2]{2,1,0:T(1,128)}), s32[16,1,2]{2,1,0:T(1,128)S(1)}, u32[]{:S(2)}, u32[]{:S(2)}) async-start(s32[16,1,2]{2,1,0:T(1,128)} %bitcast.14), calls=%async_computation | async-start | bytes 16384 | tf_op jit(solution)/shard_map/all_to_all | solution.py:83
  57.6 26.2 %copy-start.2 = (bf16[32,1280]{1,0:T(8,128)(2,1)S(1)}, bf16[32,1280]{1,0:T(8,128)(2,1)}, u32[]{:S(2)}) copy-start(bf16[32,1280]{1,0:T(8,128)(2,1)} %param.15) | copy-start | bytes 245764
  80.6 5.7 %copy-start.1 = (bf16[1280,512]{1,0:T(8,128)(2,1)S(1)}, bf16[1280,512]{1,0:T(8,128)(2,1)}, u32[]{:S(2)}) copy-start(bf16[1280,512]{1,0:T(8,128)(2,1)} %param.19) | copy-start | bytes 3932164
  85.7 0.6 copy-start.3
  88.1 9.6 %all-to-all-start.1 = ((bf16[16,2,512]{2,1,0:T(2,128)(2,1)}), bf16[16,2,512]{2,1,0:T(2,128)(2,1)S(1)}, u32[]{:S(2)}, u32[]{:S(2)}) async-start(bf16[16,2,512]{2,1,0:T(2,128)(2,1)} %broadcast_select_fusion), calls=%async_computation.1 | async-start | bytes 65536 | tf_op jit(solution)/shard_map/all_to_all | solution.py:87
  91.7 49.6 %all-gather.5.cloned.1.call-start = ((), (), s32[]{:S(2)}) async-start(), calls=%async_computation.3 | async-start | bytes 2228224 | tf_op jit(solution)/shard_map/all_gather | solution.py:97
  147.7 23.3 %copy-start.4 = (bf16[256,512]{1,0:T(8,128)(2,1)S(1)}, bf16[256,512]{1,0:T(8,128)(2,1)}, u32[]{:S(2)}) copy-start(bf16[256,512]{1,0:T(8,128)(2,1)} %param.23) | copy-start | bytes 786436
Sparse Core Ops, SparseCore 0:
  13.7 41.3 all-gather.2
  102.1 39.1 all-gather.4
where the time goes:
time: 185 us; the launch traced here: 184 us
  waiting for transfers between devices  76.8 us (42%)
  matrix products  54.5 us (29%)
  local copies, waits for them, and re-layouts  17.4 us (9%)
  between operations  14.3 us (8%)
  starting transfers between devices  11.1 us (6%)
  other arithmetic  9.36 us (5%)
    all_gather x1, waiting for transfers between devices, on_device(): lax.all_gather(dec_act[:, dec_width:], 'seq', axis=0, tiled=True)  39.2 us
    all_gather x1, waiting for transfers between devices, on_device(): lax.all_gather(enc_act[:, enc_width:], 'seq', axis=0, tiled=True)  26.7 us
    dot_general x16, matrix products, one_head(): jnp.dot(weights, value_part, preferred_element_type=jnp.float32)  23.7 us
    dot_general x16, matrix products, one_head(): lax.dot_general(query_part, key_part, (((1,), (1,)), ((), ())), preferred...  18 us
    all_to_all x1, starting transfers between devices, on_device(): lax.all_to_all(requests, 'seq', split_axis=0, concat_axis=0, tiled=True)  7.32 us
    all_to_all x1, waiting for transfers between devices, on_device(): lax.all_to_all(answers, 'seq', split_axis=0, concat_axis=0, tiled=True)  5.85 us
    dot_general x1, matrix products, on_device(): jnp.dot(hidden, shrink_weight, preferred_element_type=jnp.float32)  5.28 us
    all_to_all x1, waiting for transfers between devices, on_device(): lax.all_to_all(requests, 'seq', split_axis=0, concat_axis=0, tiled=True)  5 us
  transfers between devices with their start and end apart: 4, of which 4 were waited for; matrix products, arithmetic and copies ran while one was open for 1% of the time, Pallas kernels for 0%

commit v1 on v0

--- a/solution.py
+++ b/solution.py
@@ -1,6 +1,10 @@
+import functools
+
 import jax
 import jax.numpy as jnp
 from jax import lax
+from jax.experimental import pallas as pl
+from jax.experimental.pallas import tpu as pltpu
 from jax.sharding import PartitionSpec as P
 
 EH = 8
@@ -35,7 +39,7 @@
     return result.transpose(1, 0, 2).reshape(total, width)
 
 
-def on_device(
+def on_device_plain(
     visible_tokens,
     restore_order,
     encoder_project,
@@ -111,6 +115,315 @@
     return (latent, decoded)
 
 
+BF = jnp.bfloat16
+F32 = jnp.float32
+MESH = pl.DeviceIdType.MESH
+LOG2E = 1.4426950408889634
+
+
+def matmul(left, right):
+    return jnp.dot(left, right, preferred_element_type=F32)
+
+
+def matmul_nt(left, right):
+    return lax.dot_general(left, right, (((1,), (1,)), ((), ())), preferred_element_type=F32)
+
+
+def erf(value):
+    value = jnp.clip(value, -3.832506856900711, 3.832506856900711)
+    square = value * value
+    top = jnp.full_like(value, 0.00022905065861350646)
+    for coef in (0.0034082910107109506, 0.050955695062380861, 0.18520832239976145, 1.128379143519084):
+        top = top * square + coef
+    low = jnp.full_like(value, -1.1791602954361697e-7)
+    for coef in (
+        0.000023547966471313185,
+        0.0010179625278914885,
+        0.014070470171167667,
+        0.11098505178285362,
+        0.49746925110067538,
+        1.0,
+    ):
+        low = low * square + coef
+    return value * top / low
+
+
+def lane_heads(rows, width, heads):
+    lane = lax.broadcasted_iota(jnp.int32, (rows, width), 1)
+    size = width // heads
+    return [(lane >= h * size) & (lane < (h + 1) * size) for h in range(heads)]
+
+
+def spread_heads(queries, heads):
+    wide = queries.astype(F32)
+    masks = lane_heads(*queries.shape, heads)
+    return jnp.concatenate([jnp.where(mask, wide, 0.0).astype(BF) for mask in masks], axis=0)
+
+
+def gather_heads(stacked, heads):
+    rows, width = stacked.shape[0] // heads, stacked.shape[1]
+    masks = lane_heads(rows, width, heads)
+    total = jnp.zeros((rows, width), F32)
+    for h, mask in enumerate(masks):
+        total = jnp.where(mask, stacked[h * rows : (h + 1) * rows], total)
+    return total.astype(BF)
+
+
+class Gather:
+    def __init__(self, buf, send, recv):
+        self.buf, self.send, self.recv = buf, send, recv
+        me = lax.axis_index("seq")
+        self.group = lax.axis_index("groups")
+        core = lax.rem(me, 2)
+        x = lax.rem(lax.div(me, 2), 2)
+        low = lax.rem(lax.div(me, 4), 2)
+        high = lax.div(me, 8)
+
+        def place(flip_high, flip_low, flip_x, flip_core):
+            a = 1 - high if flip_high else high
+            b = 1 - low if flip_low else low
+            c = 1 - x if flip_x else x
+            d = 1 - core if flip_core else core
+            return a * 8 + b * 4 + c * 2 + d
+
+        self.line = [place(k // 2, k % 2, 0, 0) for k in range(4)]
+        self.line_x = [place(k // 2, k % 2, 1, 0) for k in range(4)]
+        self.other = [place(k // 2, k % 2, q, 1) for q in range(2) for k in range(4)]
+        self.me, self.x_peer, self.core_peer = me, self.line_x[0], self.other[0]
+        self.peers = self.line[1:] + [self.x_peer, self.core_peer]
+        self.started = []
+
+    def copy(self, block, slot, peer):
+        return pltpu.make_async_remote_copy(
+            src_ref=self.buf.at[block],
+            dst_ref=self.buf.at[block],
+            send_sem=self.send.at[slot],
+            recv_sem=self.recv.at[block],
+            device_id=(self.group, peer),
+            device_id_type=MESH,
+        )
+
+    def push(self, block, peer):
+        copy = self.copy(block, len(self.started), peer)
+        copy.start()
+        self.started.append(copy)
+
+    def arrive(self, block):
+        self.copy(block, 0, self.core_peer).wait_recv()
+
+    def start(self):
+        for k in (3, 2, 1):
+            self.push(self.me, self.line[k])
+        self.push(self.me, self.x_peer)
+        self.push(self.me, self.core_peer)
+
+    def forward(self):
+        for k in (1, 2, 3):
+            self.arrive(self.line[k])
+            self.push(self.line[k], self.x_peer)
+            self.push(self.line[k], self.core_peer)
+
+    def forward_x(self):
+        for k in range(4):
+            self.arrive(self.line_x[k])
+            self.push(self.line_x[k], self.core_peer)
+
+    def finish(self):
+        for block in self.other:
+            self.arrive(block)
+
+    def sent(self):
+        for copy in self.started:
+            copy.wait_send()
+
+
+def softmax_part(scores, factor):
+    highest = jnp.max(scores, -1, keepdims=True)
+    powers = jnp.exp2((scores - highest) * factor)
+    return highest, powers.astype(BF), jnp.sum(powers, -1, keepdims=True)
+
+
+def kernel(
+    tokens, order, enc_proj, enc_out, embed, mask, pos, dec_proj, dec_out, expand, shrink,
+    latent_out, decoded_out,
+    w_enc, w_eo, w_emb, w_dec, w_do, w_ex, w_sh,
+    kv, xb, eb, din, load_sem,
+    kv_send, kv_recv, x_send, x_recv, e_send, e_recv,
+):
+    peers, vis, enc2 = kv.shape
+    enc_width = enc2 // 2
+    dec_width = w_do.shape[0]
+    rows = pos.shape[0]
+    hid = rows - vis
+    visible_count = peers * vis
+
+    g_kv = Gather(kv, kv_send, kv_recv)
+    g_x = Gather(xb, x_send, x_recv)
+    g_e = Gather(eb, e_send, e_recv)
+
+    loads = [
+        pltpu.make_async_copy(enc_proj.at[:, pl.ds(enc_width, enc2)], w_enc.at[:, pl.ds(enc_width, enc2)], load_sem.at[0]),
+        pltpu.make_async_copy(dec_proj, w_dec, load_sem.at[1]),
+        pltpu.make_async_copy(enc_proj.at[:, pl.ds(0, enc_width)], w_enc.at[:, pl.ds(0, enc_width)], load_sem.at[2]),
+        pltpu.make_async_copy(enc_out, w_eo, load_sem.at[3]),
+        pltpu.make_async_copy(embed, w_emb, load_sem.at[4]),
+        pltpu.make_async_copy(dec_out, w_do, load_sem.at[5]),
+        pltpu.make_async_copy(expand, w_ex, load_sem.at[6]),
+        pltpu.make_async_copy(shrink, w_sh, load_sem.at[7]),
+    ]
+    loads[0].start()
+    loads[1].start()
+
+    barrier = pltpu.get_barrier_semaphore()
+    for peer in g_kv.peers:
+        pl.semaphore_signal(barrier, inc=1, device_id=(g_kv.group, peer), device_id_type=MESH)
+
+    me = g_kv.me
+    normed = normalize(tokens[...])
+    loads[0].wait()
+    kv[me] = matmul(normed, w_enc[:, enc_width:]).astype(BF)
+    pl.semaphore_wait(barrier, len(g_kv.peers))
+    g_kv.start()
+    for load in loads[2:]:
+        load.start()
+
+    row_id = lax.broadcasted_iota(jnp.int32, (rows, rows), 0)
+    col_id = lax.broadcasted_iota(jnp.int32, (rows, rows), 1)
+    eye = row_id == col_id
+    order_row = jnp.broadcast_to(order[...].astype(F32), (rows, rows))
+    order_col = jnp.sum(jnp.where(eye, order_row, 0.0), axis=1, keepdims=True)
+    seen_col = jnp.broadcast_to(order_col, (rows, rows)) < visible_count
+    before = jnp.sum(jnp.where((row_id < col_id) & seen_col, 1.0, 0.0), axis=0, keepdims=True)
+    before = jnp.broadcast_to(before, (rows, rows))
+    slot = jnp.where(order_row < visible_count, before, vis + col_id.astype(F32) - before)
+    to_slot = jnp.where(row_id.astype(F32) == slot, 1.0, 0.0)
+    slot_col = jnp.sum(jnp.where(eye, slot, 0.0), axis=1, keepdims=True)
+    from_slot = jnp.where(col_id.astype(F32) == slot_col, 1.0, 0.0).astype(BF)
+    ranks = jnp.sum(to_slot * order_row, axis=1, keepdims=True)[:vis].astype(jnp.int32)
+    ranks = jnp.broadcast_to(ranks, (vis, 128))
+    upper = lax.div(ranks, 16)
+    lower = (ranks - upper * 16).astype(F32).astype(BF)
+    upper = upper.astype(F32).astype(BF)
+
+    pos_slot = matmul(to_slot.astype(BF), pos[...])
+    dec_hid = (pos_slot[vis:] + mask[...].astype(F32)).astype(BF)
+    loads[1].wait()
+    act_hid = matmul(normalize(dec_hid), w_dec[...]).astype(BF)
+    xb[me, 0:vis, :] = pos_slot[:vis].astype(BF)
+    xb[me, vis:rows, :] = act_hid[:, dec_width:]
+    half = vis // 2
+    xb[me, rows : rows + half, 0:128] = upper[:half]
+    xb[me, rows : rows + half, 128:256] = upper[half:]
+    xb[me, rows : rows + half, 256:384] = lower[:half]
+    xb[me, rows : rows + half, 384:512] = lower[half:]
+    g_x.start()
+
+    loads[2].wait()
+    enc_q = spread_heads(matmul(normed, w_enc[:, :enc_width]).astype(BF), EH)
+    dec_qh = spread_heads(act_hid[:, :dec_width], DH)
+
+    g_kv.forward()
+    g_kv.forward_x()
+    g_kv.finish()
+    pairs = kv[...].reshape(visible_count, enc2)
+    scores = matmul_nt(enc_q, pairs[:, :enc_width])
+    _, powers, total = softmax_part(scores, (enc_width // EH) ** (-0.5) * LOG2E)
+    mix = gather_heads(matmul(powers, pairs[:, enc_width:]) / total, EH)
+    loads[3].wait()
+    latent = (tokens[...].astype(F32) + matmul(mix, w_eo[...])).astype(BF)
+    latent_out[...] = latent
+    loads[4].wait()
+    eb[me] = matmul(normalize(latent), w_emb[...]).astype(BF)
+    g_e.start()
+
+    g_x.forward()
+    g_x.forward_x()
+    g_x.finish()
+    factor = (dec_width // DH) ** (-0.5) * LOG2E
+    g_e.forward()
+    g_e.forward_x()
+    hid_keys = xb[:, vis:rows, 0:dec_width].reshape(peers * hid, dec_width)
+    hid_values = xb[:, vis:rows, dec_width : 2 * dec_width].reshape(peers * hid, dec_width)
+    top_hh, pow_hh, sum_hh = softmax_part(matmul_nt(dec_qh, hid_keys), factor)
+    acc_hh = matmul(pow_hh, hid_values)
+
+    g_e.finish()
+    rank_hi = jnp.concatenate(
+        [xb[:, rows : rows + half, 0:128].astype(F32), xb[:, rows : rows + half, 128:256].astype(F32)], axis=1
+    ).reshape(visible_count, 128)
+    rank_lo = jnp.concatenate(
+        [xb[:, rows : rows + half, 256:384].astype(F32), xb[:, rows : rows + half, 384:512].astype(F32)], axis=1
+    ).reshape(visible_count, 128)
+    rank = rank_hi * 16.0 + rank_lo
+    lane = lax.broadcasted_iota(jnp.int32, (visible_count, 128), 1).astype(F32)
+    hot = jnp.concatenate(
+        [jnp.where(rank == lane + 128.0 * k, 1.0, 0.0).astype(BF) for k in range(visible_count // 128)], axis=1
+    )
+    width = eb.shape[2]
+    picked = matmul(hot, eb[...].reshape(visible_count, width))
+    dec_vis = (picked + xb[:, 0:vis, :].reshape(visible_count, width).astype(F32)).astype(BF)
+    din[...] = dec_vis.reshape(peers, vis, width)
+    pairs_vis = matmul(normalize(dec_vis), w_dec[:, dec_width:]).astype(BF)
+    own_vis = din[me]
+    dec_qv = spread_heads(matmul(normalize(own_vis), w_dec[:, :dec_width]).astype(BF), DH)
+    vis_keys, vis_values = pairs_vis[:, :dec_width], pairs_vis[:, dec_width:]
+
+    def merge(scores, top, total, acc):
+        highest = jnp.maximum(top, jnp.max(scores, -1, keepdims=True))
+        powers = jnp.exp2((scores - highest) * factor)
+        fade = jnp.exp2((top - highest) * factor)
+        total = total * fade + jnp.sum(powers, -1, keepdims=True)
+        return (acc * fade + matmul(powers.astype(BF), vis_values)) / total
+
+    mix_h = gather_heads(merge(matmul_nt(dec_qh, vis_keys), top_hh, sum_hh, acc_hh), DH)
+    top_vh, pow_vh, sum_vh = softmax_part(matmul_nt(dec_qv, hid_keys), factor)
+    acc_vh = matmul(pow_vh, hid_values)
+    mix_v = gather_heads(merge(matmul_nt(dec_qv, vis_keys), top_vh, sum_vh, acc_vh), DH)
+
+    dec_in = jnp.concatenate([own_vis, dec_hid], axis=0)
+    dec_mix = jnp.concatenate([mix_v, mix_h], axis=0)
+    loads[5].wait()
+    middle = (dec_in.astype(F32) + matmul(dec_mix, w_do[...])).astype(BF)
+    loads[6].wait()
+    wide = matmul(normalize(middle), w_ex[...])
+    hidden = (0.5 * wide * (1.0 + erf(wide * 0.7071067811865476))).astype(BF)
+    loads[7].wait()
+    decoded = (middle.astype(F32) + matmul(hidden, w_sh[...])).astype(BF)
+    decoded_out[...] = matmul(from_slot, decoded).astype(BF)
+    g_kv.sent()
+    g_x.sent()
+    g_e.sent()
+
+
+def on_device(peers, tokens, order, enc_proj, enc_out, embed, mask, pos, dec_proj, dec_out, expand, shrink):
+    vis, rows, width = tokens.shape[0], pos.shape[0], pos.shape[1]
+    weights = (enc_proj, enc_out, embed, dec_proj, dec_out, expand, shrink)
+    vmem = pl.BlockSpec(memory_space=pltpu.VMEM)
+    anywhere = pl.BlockSpec(memory_space=pl.ANY)
+    return pl.pallas_call(
+        kernel,
+        out_shape=(
+            jax.ShapeDtypeStruct(tokens.shape, BF),
+            jax.ShapeDtypeStruct(pos.shape, BF),
+        ),
+        in_specs=[vmem, vmem, anywhere, anywhere, anywhere, vmem, vmem, anywhere, anywhere, anywhere, anywhere],
+        out_specs=(vmem, vmem),
+        scratch_shapes=[pltpu.VMEM(w.shape, BF) for w in weights]
+        + [
+            pltpu.VMEM((peers, vis, 2 * enc_out.shape[0]), BF),
+            pltpu.VMEM((peers, rows + vis // 2, width), BF),
+            pltpu.VMEM((peers, vis, width), BF),
+            pltpu.VMEM((peers, vis, width), BF),
+            pltpu.SemaphoreType.DMA((8,)),
+        ]
+        + [pltpu.SemaphoreType.DMA((n,)) for _ in range(3) for n in (15, peers)],
+        compiler_params=pltpu.CompilerParams(
+            collective_id=0, has_side_effects=True, vmem_limit_bytes=56 * 1024 * 1024
+        ),
+    )(tokens, order.reshape(1, rows), enc_proj, enc_out, embed, mask.reshape(1, width), pos,
+      dec_proj, dec_out, expand, shrink)
+
+
 def solution(mesh):
     in_specs = (
         P(("groups", "seq"), None),
@@ -126,6 +439,8 @@
         P(),
     )
     out_specs = (P(("groups", "seq"), None), P(("groups", "seq"), None))
+    peers = mesh.shape["seq"]
+    body = functools.partial(on_device, peers) if peers == 16 else on_device_plain
     return jax.shard_map(
-        on_device, mesh=mesh, in_specs=in_specs, out_specs=out_specs, check_vma=False
+        body, mesh=mesh, in_specs=in_specs, out_specs=out_specs, check_vma=False
     )

time: 185 us -> 61.3 us (0.33)
  waiting for transfers between devices: 76.8 us -> 0 us
  Pallas kernels: 0 us -> 55.3 us
  matrix products: 54.5 us -> 0 us
  between operations: 14.3 us -> 0.64 us
  local copies, waits for them, and re-layouts: 17.4 us -> 4.35 us
  starting transfers between devices: 11.1 us -> 0 us
  other arithmetic: 9.36 us -> 0 us
    all_gather x2 -> x0, waiting for transfers between devices: 65.9 us -> none  [the longest x1 39.2 us: on_device(): lax.all_gather(dec_act[:, dec_width:], 'seq', axis=0, tiled=True)]
    pallas_call x0 -> x1, Pallas kernels: none -> 55.3 us  [on_device(): pl.pallas_call(kernel, out_shape=(jax.ShapeDtypeStruct(tokens.shape, BF),...]
    dot_general x38 -> x0, matrix products: 54.5 us -> none  [the longest x16 23.7 us: one_head(): jnp.dot(weights, value_part, preferred_element_type=jnp.float32)]
    all_to_all x2 -> x0, starting transfers between devices: 11 us -> none  [the longest x1 7.32 us: on_device(): lax.all_to_all(requests, 'seq', split_axis=0, concat_axis=0, tiled=True)]
    all_to_all x2 -> x0, waiting for transfers between devices: 10.9 us -> none  [the longest x1 5.85 us: on_device(): lax.all_to_all(answers, 'seq', split_axis=0, concat_axis=0, tiled=True)]
    slice x11 -> x0, local copies, waits for them, and re-layouts: 10.6 us -> none  [the longest x2 4.94 us: on_device(): dec_pairs[:, dec_width:]]
    reduce_sum x23 -> x0, other arithmetic: 8.11 us -> none  [the longest x16 4.03 us: one_head(): weights = (powers / jnp.sum(powers, -1, keepdims=True)).astype(jnp.bfloat16)]
    unnamed x14 -> x2, local copies, waits for them, and re-layouts: 0.46 us -> 3.09 us
  transfers between devices with their start and end apart: 4 -> 0, of which waited for: 4 -> 0; matrix products, arithmetic and copies ran while one was open for 1% -> 0% of each run, Pallas kernels for 0% -> 0%
where the time goes in v1:
time: 61.3 us; the launch traced here: 60.3 us
  Pallas kernels  55.3 us (90%)
  local copies, waits for them, and re-layouts  4.35 us (7%)
  between operations  0.64 us (1%)
    pallas_call x1, Pallas kernels, on_device(): pl.pallas_call(kernel, out_shape=(jax.ShapeDtypeStruct(tokens.shape, BF),...  55.3 us
    unnamed x2, local copies, waits for them, and re-layouts  3.09 us
    reshape x1, local copies, waits for them, and re-layouts, on_device(): mask.reshape(1, width)  1.26 us

profile of v1, /device:TPU:1, one launch (start us, length us, event | category | flops | bytes accessed | tf_op | source)
XLA Modules:
  0.0 60.3 jit_solution(10519098989547905504)
XLA Ops:
  0.6 1.3 %reshape.11.mask = bf16[1,512]{1,0:T(2,128)(2,1)} reshape(bf16[512]{0:T(512)(128)(2,1)} %param.16) | data formatting | bytes 2048 | tf_op jit(solution)/shard_map/reshape | solution.py:423
  1.9 55.3 %shard_map.122 = (bf16[32,1280]{1,0:T(8,128)(2,1)}, bf16[128,512]{1,0:T(8,128)(2,1)}) custom-call(bf16[32,1280]{1,0:T(8,128)(2,1)} %tokens.1, s32[1,128]{1,0:T(1,128)} %bitcast.1, bf16[1280,1920]{1,0:T(8,128)(2,1)} %enc_proj.1, bf16[640,1280]{1,0:T(8,128)(2,1)} %enc_out.1, bf16[1280,512]{1,0:T(8,128)(2,1)} %embed.1, bf16[1,512]{1,0:T(2,128)(2,1)} %reshape.11.mask, ...), custom_call_target="tpu_custom_call" | custom-call | tf_op jit(solution)/shard_map/pallas_call | solution.py:403
  57.2 1.5 %copy.15 = bf16[32,1280]{1,0:T(8,128)(2,1)} copy(bf16[32,1280]{1,0:T(8,128)(2,1)} %get-tuple-element.4) | data formatting | bytes 163840
  58.7 1.6 %copy.16 = bf16[128,512]{1,0:T(8,128)(2,1)} copy(bf16[128,512]{1,0:T(8,128)(2,1)} %get-tuple-element.5) | data formatting | bytes 262144

commit v2 on v1

--- a/solution.py
+++ b/solution.py
@@ -217,8 +217,8 @@
         self.push(self.me, self.x_peer)
         self.push(self.me, self.core_peer)
 
-    def forward(self):
-        for k in (1, 2, 3):
+    def forward(self, steps=(1, 2, 3)):
+        for k in steps:
             self.arrive(self.line[k])
             self.push(self.line[k], self.x_peer)
             self.push(self.line[k], self.core_peer)
@@ -247,45 +247,40 @@
     tokens, order, enc_proj, enc_out, embed, mask, pos, dec_proj, dec_out, expand, shrink,
     latent_out, decoded_out,
     w_enc, w_eo, w_emb, w_dec, w_do, w_ex, w_sh,
-    kv, xb, eb, din, load_sem,
-    kv_send, kv_recv, x_send, x_recv, e_send, e_recv,
+    tb, xb, eb, din, load_sem,
+    t_send, t_recv, x_send, x_recv, e_send, e_recv,
 ):
-    peers, vis, enc2 = kv.shape
-    enc_width = enc2 // 2
+    peers, vis, _ = tb.shape
+    enc_width = w_eo.shape[0]
+    enc2 = 2 * enc_width
     dec_width = w_do.shape[0]
     rows = pos.shape[0]
     hid = rows - vis
     visible_count = peers * vis
 
-    g_kv = Gather(kv, kv_send, kv_recv)
+    g_t = Gather(tb, t_send, t_recv)
     g_x = Gather(xb, x_send, x_recv)
     g_e = Gather(eb, e_send, e_recv)
 
     loads = [
-        pltpu.make_async_copy(enc_proj.at[:, pl.ds(enc_width, enc2)], w_enc.at[:, pl.ds(enc_width, enc2)], load_sem.at[0]),
-        pltpu.make_async_copy(dec_proj, w_dec, load_sem.at[1]),
-        pltpu.make_async_copy(enc_proj.at[:, pl.ds(0, enc_width)], w_enc.at[:, pl.ds(0, enc_width)], load_sem.at[2]),
-        pltpu.make_async_copy(enc_out, w_eo, load_sem.at[3]),
-        pltpu.make_async_copy(embed, w_emb, load_sem.at[4]),
-        pltpu.make_async_copy(dec_out, w_do, load_sem.at[5]),
-        pltpu.make_async_copy(expand, w_ex, load_sem.at[6]),
-        pltpu.make_async_copy(shrink, w_sh, load_sem.at[7]),
+        pltpu.make_async_copy(dec_proj, w_dec, load_sem.at[0]),
+        pltpu.make_async_copy(enc_proj, w_enc, load_sem.at[1]),
+        pltpu.make_async_copy(enc_out, w_eo, load_sem.at[2]),
+        pltpu.make_async_copy(embed, w_emb, load_sem.at[3]),
+        pltpu.make_async_copy(dec_out, w_do, load_sem.at[4]),
+        pltpu.make_async_copy(expand, w_ex, load_sem.at[5]),
+        pltpu.make_async_copy(shrink, w_sh, load_sem.at[6]),
     ]
-    loads[0].start()
-    loads[1].start()
-
     barrier = pltpu.get_barrier_semaphore()
-    for peer in g_kv.peers:
-        pl.semaphore_signal(barrier, inc=1, device_id=(g_kv.group, peer), device_id_type=MESH)
-
-    me = g_kv.me
-    normed = normalize(tokens[...])
-    loads[0].wait()
-    kv[me] = matmul(normed, w_enc[:, enc_width:]).astype(BF)
-    pl.semaphore_wait(barrier, len(g_kv.peers))
-    g_kv.start()
-    for load in loads[2:]:
+    for peer in g_t.peers:
+        pl.semaphore_signal(barrier, inc=1, device_id=(g_t.group, peer), device_id_type=MESH)
+    for load in loads:
         load.start()
+
+    me = g_t.me
+    tb[me] = tokens[...]
+    pl.semaphore_wait(barrier, len(g_t.peers))
+    g_t.start()
 
     row_id = lax.broadcasted_iota(jnp.int32, (rows, rows), 0)
     col_id = lax.broadcasted_iota(jnp.int32, (rows, rows), 1)
@@ -306,8 +301,8 @@
     upper = upper.astype(F32).astype(BF)
 
     pos_slot = matmul(to_slot.astype(BF), pos[...])
-    dec_hid = (pos_slot[vis:] + mask[...].astype(F32)).astype(BF)
-    loads[1].wait()
+    dec_hid = (pos_slot[vis:] + mask[...].astype(F32).reshape(1, -1)).astype(BF)
+    loads[0].wait()
     act_hid = matmul(normalize(dec_hid), w_dec[...]).astype(BF)
     xb[me, 0:vis, :] = pos_slot[:vis].astype(BF)
     xb[me, vis:rows, :] = act_hid[:, dec_width:]
@@ -316,32 +311,45 @@
     xb[me, rows : rows + half, 128:256] = upper[half:]
     xb[me, rows : rows + half, 256:384] = lower[:half]
     xb[me, rows : rows + half, 384:512] = lower[half:]
-    g_x.start()
-
-    loads[2].wait()
-    enc_q = spread_heads(matmul(normed, w_enc[:, :enc_width]).astype(BF), EH)
+    g_x.push(me, g_x.x_peer)
+    g_x.push(me, g_x.line[1])
+
+    def pairs_of(blocks):
+        rows_in = jnp.concatenate([tb[block] for block in blocks], axis=0)
+        return matmul(normalize(rows_in), w_enc[:, enc_width:]).astype(BF)
+
+    loads[1].wait()
+    enc_q = spread_heads(matmul(normalize(tokens[...]), w_enc[:, :enc_width]).astype(BF), EH)
     dec_qh = spread_heads(act_hid[:, :dec_width], DH)
 
-    g_kv.forward()
-    g_kv.forward_x()
-    g_kv.finish()
-    pairs = kv[...].reshape(visible_count, enc2)
+    g_t.forward()
+    g_x.push(me, g_x.line[2])
+    g_x.push(me, g_x.core_peer)
+    pairs = [pairs_of(g_t.line)]
+    g_t.forward_x()
+    g_x.push(me, g_x.line[3])
+    pairs.append(pairs_of(g_t.line_x))
+    g_x.forward((1,))
+    g_t.finish()
+    pairs.append(pairs_of(g_t.other))
+    g_x.forward((2,))
+    pairs = jnp.concatenate(pairs, axis=0)
     scores = matmul_nt(enc_q, pairs[:, :enc_width])
     _, powers, total = softmax_part(scores, (enc_width // EH) ** (-0.5) * LOG2E)
     mix = gather_heads(matmul(powers, pairs[:, enc_width:]) / total, EH)
-    loads[3].wait()
+    loads[2].wait()
     latent = (tokens[...].astype(F32) + matmul(mix, w_eo[...])).astype(BF)
     latent_out[...] = latent
-    loads[4].wait()
+    loads[3].wait()
     eb[me] = matmul(normalize(latent), w_emb[...]).astype(BF)
     g_e.start()
 
-    g_x.forward()
+    g_x.forward((3,))
+    g_e.forward()
+    g_e.forward_x()
     g_x.forward_x()
     g_x.finish()
     factor = (dec_width // DH) ** (-0.5) * LOG2E
-    g_e.forward()
-    g_e.forward_x()
     hid_keys = xb[:, vis:rows, 0:dec_width].reshape(peers * hid, dec_width)
     hid_values = xb[:, vis:rows, dec_width : 2 * dec_width].reshape(peers * hid, dec_width)
     top_hh, pow_hh, sum_hh = softmax_part(matmul_nt(dec_qh, hid_keys), factor)
@@ -382,15 +390,15 @@
 
     dec_in = jnp.concatenate([own_vis, dec_hid], axis=0)
     dec_mix = jnp.concatenate([mix_v, mix_h], axis=0)
+    loads[4].wait()
+    middle = (dec_in.astype(F32) + matmul(dec_mix, w_do[...])).astype(BF)
     loads[5].wait()
-    middle = (dec_in.astype(F32) + matmul(dec_mix, w_do[...])).astype(BF)
-    loads[6].wait()
     wide = matmul(normalize(middle), w_ex[...])
     hidden = (0.5 * wide * (1.0 + erf(wide * 0.7071067811865476))).astype(BF)
-    loads[7].wait()
+    loads[6].wait()
     decoded = (middle.astype(F32) + matmul(hidden, w_sh[...])).astype(BF)
     decoded_out[...] = matmul(from_slot, decoded).astype(BF)
-    g_kv.sent()
+    g_t.sent()
     g_x.sent()
     g_e.sent()
 
@@ -410,17 +418,17 @@
         out_specs=(vmem, vmem),
         scratch_shapes=[pltpu.VMEM(w.shape, BF) for w in weights]
         + [
-            pltpu.VMEM((peers, vis, 2 * enc_out.shape[0]), BF),
+            pltpu.VMEM((peers, vis, tokens.shape[1]), BF),
             pltpu.VMEM((peers, rows + vis // 2, width), BF),
             pltpu.VMEM((peers, vis, width), BF),
             pltpu.VMEM((peers, vis, width), BF),
-            pltpu.SemaphoreType.DMA((8,)),
+            pltpu.SemaphoreType.DMA((7,)),
         ]
         + [pltpu.SemaphoreType.DMA((n,)) for _ in range(3) for n in (15, peers)],
         compiler_params=pltpu.CompilerParams(
             collective_id=0, has_side_effects=True, vmem_limit_bytes=56 * 1024 * 1024
         ),
-    )(tokens, order.reshape(1, rows), enc_proj, enc_out, embed, mask.reshape(1, width), pos,
+    )(tokens, order.reshape(1, rows), enc_proj, enc_out, embed, mask, pos,
       dec_proj, dec_out, expand, shrink)
 
 

time: 61.3 us -> 50.1 us (0.82); the launches traced: 60.3 us -> 49.9 us
  Pallas kernels: 55.3 us -> 46.2 us
  local copies, waits for them, and re-layouts: 4.35 us -> 3.09 us
    pallas_call x1, Pallas kernels: 55.3 us -> 46.2 us  [on_device(): pl.pallas_call(kernel, out_shape=(jax.ShapeDtypeStruct(tokens.shape, BF),...]
    reshape x1 -> x0, local copies, waits for them, and re-layouts: 1.26 us -> none  [on_device(): mask.reshape(1, width)]
where the time goes in v2:
time: 50.1 us; the launch traced here: 49.9 us
  Pallas kernels  46.2 us (92%)
  local copies, waits for them, and re-layouts  3.09 us (6%)
  between operations  0.64 us (1%)
    pallas_call x1, Pallas kernels, on_device(): pl.pallas_call(kernel, out_shape=(jax.ShapeDtypeStruct(tokens.shape, BF),...  46.2 us
    unnamed x2, local copies, waits for them, and re-layouts  3.09 us

profile of v2, /device:TPU:1, one launch (start us, length us, event | category | flops | bytes accessed | tf_op | source)
XLA Modules:
  0.0 49.9 jit_solution(3472700702151531274)
XLA Ops:
  0.6 46.2 %shard_map.122 = (bf16[32,1280]{1,0:T(8,128)(2,1)}, bf16[128,512]{1,0:T(8,128)(2,1)}) custom-call(bf16[32,1280]{1,0:T(8,128)(2,1)} %tokens.1, s32[1,128]{1,0:T(1,128)} %bitcast.1, bf16[1280,1920]{1,0:T(8,128)(2,1)} %enc_proj.1, bf16[640,1280]{1,0:T(8,128)(2,1)} %enc_out.1, bf16[1280,512]{1,0:T(8,128)(2,1)} %embed.1, bf16[512]{0:T(512)(128)(2,1)} %mask.1, ...), custom_call_target="tpu_custom_call" | custom-call | tf_op jit(solution)/shard_map/pallas_call | solution.py:411
  46.8 1.5 %copy.15 = bf16[32,1280]{1,0:T(8,128)(2,1)} copy(bf16[32,1280]{1,0:T(8,128)(2,1)} %get-tuple-element.4) | data formatting | bytes 163840
  48.3 1.6 %copy.16 = bf16[128,512]{1,0:T(8,128)(2,1)} copy(bf16[128,512]{1,0:T(8,128)(2,1)} %get-tuple-element.5) | data formatting | bytes 262144

commit v3 on v2

--- a/solution.py
+++ b/solution.py
@@ -212,9 +212,9 @@
         self.copy(block, 0, self.core_peer).wait_recv()
 
     def start(self):
-        for k in (3, 2, 1):
+        self.push(self.me, self.x_peer)
+        for k in (1, 2, 3):
             self.push(self.me, self.line[k])
-        self.push(self.me, self.x_peer)
         self.push(self.me, self.core_peer)
 
     def forward(self, steps=(1, 2, 3)):
@@ -336,6 +336,7 @@
     pairs = jnp.concatenate(pairs, axis=0)
     scores = matmul_nt(enc_q, pairs[:, :enc_width])
     _, powers, total = softmax_part(scores, (enc_width // EH) ** (-0.5) * LOG2E)
+    g_x.forward((3,))
     mix = gather_heads(matmul(powers, pairs[:, enc_width:]) / total, EH)
     loads[2].wait()
     latent = (tokens[...].astype(F32) + matmul(mix, w_eo[...])).astype(BF)
@@ -344,16 +345,20 @@
     eb[me] = matmul(normalize(latent), w_emb[...]).astype(BF)
     g_e.start()
 
-    g_x.forward((3,))
+    g_x.forward_x()
     g_e.forward()
-    g_e.forward_x()
-    g_x.forward_x()
     g_x.finish()
     factor = (dec_width // DH) ** (-0.5) * LOG2E
     hid_keys = xb[:, vis:rows, 0:dec_width].reshape(peers * hid, dec_width)
     hid_values = xb[:, vis:rows, dec_width : 2 * dec_width].reshape(peers * hid, dec_width)
-    top_hh, pow_hh, sum_hh = softmax_part(matmul_nt(dec_qh, hid_keys), factor)
-    acc_hh = matmul(pow_hh, hid_values)
+    middle_row = dec_qh.shape[0] // 2
+    parts = []
+    for queries in (dec_qh[:middle_row], dec_qh[middle_row:]):
+        top, powers, total = softmax_part(matmul_nt(queries, hid_keys), factor)
+        parts.append((top, total, matmul(powers, hid_values)))
+        if len(parts) == 1:
+            g_e.forward_x()
+    top_hh, sum_hh, acc_hh = (jnp.concatenate(pair, axis=0) for pair in zip(*parts))
 
     g_e.finish()
     rank_hi = jnp.concatenate(
@@ -403,12 +408,23 @@
     g_e.sent()
 
 
+def hand_out(latent, decoded, latent_out, decoded_out, sem):
+    copies = [
+        pltpu.make_async_copy(latent, latent_out, sem.at[0]),
+        pltpu.make_async_copy(decoded, decoded_out, sem.at[1]),
+    ]
+    for copy in copies:
+        copy.start()
+    for copy in copies:
+        copy.wait()
+
+
 def on_device(peers, tokens, order, enc_proj, enc_out, embed, mask, pos, dec_proj, dec_out, expand, shrink):
     vis, rows, width = tokens.shape[0], pos.shape[0], pos.shape[1]
     weights = (enc_proj, enc_out, embed, dec_proj, dec_out, expand, shrink)
     vmem = pl.BlockSpec(memory_space=pltpu.VMEM)
     anywhere = pl.BlockSpec(memory_space=pl.ANY)
-    return pl.pallas_call(
+    latent, decoded = pl.pallas_call(
         kernel,
         out_shape=(
             jax.ShapeDtypeStruct(tokens.shape, BF),
@@ -430,6 +446,13 @@
         ),
     )(tokens, order.reshape(1, rows), enc_proj, enc_out, embed, mask, pos,
       dec_proj, dec_out, expand, shrink)
+    return pl.pallas_call(
+        hand_out,
+        out_shape=(jax.ShapeDtypeStruct(tokens.shape, BF), jax.ShapeDtypeStruct(pos.shape, BF)),
+        in_specs=[anywhere, anywhere],
+        out_specs=(anywhere, anywhere),
+        scratch_shapes=[pltpu.SemaphoreType.DMA((2,))],
+    )(latent, decoded)
 
 
 def solution(mesh):

time: 50.1 us -> 54.7 us (1.092)
  Pallas kernels: 46.2 us -> 53.9 us
  local copies, waits for them, and re-layouts: 3.09 us -> 0 us
    pallas_call x0 -> x1, Pallas kernels: none -> 7.57 us  [on_device(): pl.pallas_call(hand_out, out_shape=(jax.ShapeDtypeStruct(tokens.shape, BF...]
    unnamed x2 -> x0, local copies, waits for them, and re-layouts: 3.09 us -> none
where the time goes in v3:
time: 54.7 us; the launch traced here: 54.6 us
  Pallas kernels  53.9 us (99%)
  between operations  0.64 us (1%)
    pallas_call x1, Pallas kernels, on_device(): pl.pallas_call(kernel, out_shape=(jax.ShapeDtypeStruct(tokens.shape, BF),...  46.3 us
    pallas_call x1, Pallas kernels, on_device(): pl.pallas_call(hand_out, out_shape=(jax.ShapeDtypeStruct(tokens.shape, BF...  7.57 us

profile of v3, /device:TPU:1, one launch (start us, length us, event | category | flops | bytes accessed | tf_op | source)
XLA Modules:
  0.0 54.6 jit_solution(14186787289391461614)
XLA Ops:
  0.6 46.3 %shard_map.122 = (bf16[32,1280]{1,0:T(8,128)(2,1)}, bf16[128,512]{1,0:T(8,128)(2,1)}) custom-call(bf16[32,1280]{1,0:T(8,128)(2,1)} %tokens.1, s32[1,128]{1,0:T(1,128)} %bitcast.1, bf16[1280,1920]{1,0:T(8,128)(2,1)} %enc_proj.1, bf16[640,1280]{1,0:T(8,128)(2,1)} %enc_out.1, bf16[1280,512]{1,0:T(8,128)(2,1)} %embed.1, bf16[512]{0:T(512)(128)(2,1)} %mask.1, ...), custom_call_target="tpu_custom_call" | custom-call | tf_op jit(solution)/shard_map/pallas_call | solution.py:427
  47.0 7.6 %shard_map.123 = (bf16[32,1280]{1,0:T(8,128)(2,1)}, bf16[128,512]{1,0:T(8,128)(2,1)}) custom-call(bf16[32,1280]{1,0:T(8,128)(2,1)} %get-tuple-element.4.latent, bf16[128,512]{1,0:T(8,128)(2,1)} %get-tuple-element.5.decoded), custom_call_target="tpu_custom_call" | custom-call | tf_op jit(solution)/shard_map/pallas_call | solution.py:449

commit v4 on v2

--- a/solution.py
+++ b/solution.py
@@ -346,14 +346,19 @@
 
     g_x.forward((3,))
     g_e.forward()
-    g_e.forward_x()
     g_x.forward_x()
     g_x.finish()
     factor = (dec_width // DH) ** (-0.5) * LOG2E
     hid_keys = xb[:, vis:rows, 0:dec_width].reshape(peers * hid, dec_width)
     hid_values = xb[:, vis:rows, dec_width : 2 * dec_width].reshape(peers * hid, dec_width)
-    top_hh, pow_hh, sum_hh = softmax_part(matmul_nt(dec_qh, hid_keys), factor)
-    acc_hh = matmul(pow_hh, hid_values)
+    middle_row = dec_qh.shape[0] // 2
+    parts = []
+    for queries in (dec_qh[:middle_row], dec_qh[middle_row:]):
+        top, powers, total = softmax_part(matmul_nt(queries, hid_keys), factor)
+        parts.append((top, total, matmul(powers, hid_values)))
+        if len(parts) == 1:
+            g_e.forward_x()
+    top_hh, sum_hh, acc_hh = (jnp.concatenate(pair, axis=0) for pair in zip(*parts))
 
     g_e.finish()
     rank_hi = jnp.concatenate(
@@ -408,7 +413,7 @@
     weights = (enc_proj, enc_out, embed, dec_proj, dec_out, expand, shrink)
     vmem = pl.BlockSpec(memory_space=pltpu.VMEM)
     anywhere = pl.BlockSpec(memory_space=pl.ANY)
-    return pl.pallas_call(
+    latent, decoded = pl.pallas_call(
         kernel,
         out_shape=(
             jax.ShapeDtypeStruct(tokens.shape, BF),
@@ -430,6 +435,7 @@
         ),
     )(tokens, order.reshape(1, rows), enc_proj, enc_out, embed, mask, pos,
       dec_proj, dec_out, expand, shrink)
+    return latent, decoded
 
 
 def solution(mesh):

time: 50.1 us -> 50.1 us (level)
  the two profiles are of different devices: /device:TPU:1 before, /device:TPU:0 now
where the time goes in v4:
time: 50.1 us; the launch traced here: 49.9 us
  Pallas kernels  46.2 us (92%)
  local copies, waits for them, and re-layouts  3.09 us (6%)
  between operations  0.64 us (1%)
    pallas_call x1, Pallas kernels, on_device(): pl.pallas_call(kernel, out_shape=(jax.ShapeDtypeStruct(tokens.shape, BF),...  46.2 us
    unnamed x2, local copies, waits for them, and re-layouts  3.09 us

profile of v4, /device:TPU:0, one launch (start us, length us, event | category | flops | bytes accessed | tf_op | source)
XLA Modules:
  0.0 49.9 jit_solution(3839657893896811408)
XLA Ops:
  0.6 46.2 %shard_map.122 = (bf16[32,1280]{1,0:T(8,128)(2,1)}, bf16[128,512]{1,0:T(8,128)(2,1)}) custom-call(bf16[32,1280]{1,0:T(8,128)(2,1)} %tokens.1, s32[1,128]{1,0:T(1,128)} %bitcast.1, bf16[1280,1920]{1,0:T(8,128)(2,1)} %enc_proj.1, bf16[640,1280]{1,0:T(8,128)(2,1)} %enc_out.1, bf16[1280,512]{1,0:T(8,128)(2,1)} %embed.1, bf16[512]{0:T(512)(128)(2,1)} %mask.1, ...), custom_call_target="tpu_custom_call" | custom-call | tf_op jit(solution)/shard_map/pallas_call | solution.py:416
  46.8 1.5 %copy.15 = bf16[32,1280]{1,0:T(8,128)(2,1)} copy(bf16[32,1280]{1,0:T(8,128)(2,1)} %get-tuple-element.4) | data formatting | bytes 163840
  48.4 1.6 %copy.16 = bf16[128,512]{1,0:T(8,128)(2,1)} copy(bf16[128,512]{1,0:T(8,128)(2,1)} %get-tuple-element.5) | data formatting | bytes 262144

commit v5 on v2

--- a/solution.py
+++ b/solution.py
@@ -212,9 +212,9 @@
         self.copy(block, 0, self.core_peer).wait_recv()
 
     def start(self):
-        for k in (3, 2, 1):
+        self.push(self.me, self.x_peer)
+        for k in (1, 2, 3):
             self.push(self.me, self.line[k])
-        self.push(self.me, self.x_peer)
         self.push(self.me, self.core_peer)
 
     def forward(self, steps=(1, 2, 3)):

time: 50.1 us -> 51.4 us (1.026)
  Pallas kernels: 46.2 us -> 47.5 us
    pallas_call x1, Pallas kernels: 46.2 us -> 47.5 us  [on_device(): pl.pallas_call(kernel, out_shape=(jax.ShapeDtypeStruct(tokens.shape, BF),...]
where the time goes in v5:
time: 51.4 us; the launch traced here: 51.2 us
  Pallas kernels  47.5 us (92%)
  local copies, waits for them, and re-layouts  3.09 us (6%)
  between operations  0.64 us (1%)
    pallas_call x1, Pallas kernels, on_device(): pl.pallas_call(kernel, out_shape=(jax.ShapeDtypeStruct(tokens.shape, BF),...  47.5 us
    unnamed x2, local copies, waits for them, and re-layouts  3.09 us

profile of v5, /device:TPU:1, one launch (start us, length us, event | category | flops | bytes accessed | tf_op | source)
XLA Modules:
  0.0 51.2 jit_solution(7721286588137669527)
XLA Ops:
  0.6 47.5 %shard_map.122 = (bf16[32,1280]{1,0:T(8,128)(2,1)}, bf16[128,512]{1,0:T(8,128)(2,1)}) custom-call(bf16[32,1280]{1,0:T(8,128)(2,1)} %tokens.1, s32[1,128]{1,0:T(1,128)} %bitcast.1, bf16[1280,1920]{1,0:T(8,128)(2,1)} %enc_proj.1, bf16[640,1280]{1,0:T(8,128)(2,1)} %enc_out.1, bf16[1280,512]{1,0:T(8,128)(2,1)} %embed.1, bf16[512]{0:T(512)(128)(2,1)} %mask.1, ...), custom_call_target="tpu_custom_call" | custom-call | tf_op jit(solution)/shard_map/pallas_call | solution.py:411
  48.1 1.5 %copy.15 = bf16[32,1280]{1,0:T(8,128)(2,1)} copy(bf16[32,1280]{1,0:T(8,128)(2,1)} %get-tuple-element.4) | data formatting | bytes 163840
  49.7 1.6 %copy.16 = bf16[128,512]{1,0:T(8,128)(2,1)} copy(bf16[128,512]{1,0:T(8,128)(2,1)} %get-tuple-element.5) | data formatting | bytes 262144
